TPU v7x, 256 devices: a whole 4x4x8 slice. The times are simulated.
256 devices in a mesh: depth: 16 (over x_lo, y, core), dp: 16 (over x_hi, z).
Axes of the slice: x: 4 (x_hi: 2, x_lo: 2; x = x_hi * 2 + x_lo), y: 4, z: 8, core: 2. Of those that a mesh axis runs over, the one named last changes fastest.
Arguments:
- token_ids: int32 [2048], P('dp'), may hold values from 0 to 20479
- embedding: bfloat16 [20480, 512], P('depth'), may hold values from -6 to 6
- w_up: bfloat16 [32, 512, 2048], P('depth'), may hold values from -0.25 to 0.25
- w_down: bfloat16 [32, 2048, 512], P('depth'), may hold values from -0.125 to 0.125
- cotangent: bfloat16 [2048, 512], P('dp'), may hold values from -0.119628906 to 0.119628906
Outputs:
- grad_up: float32 [32, 512, 2048], P('depth', 'dp')
- grad_down: float32 [32, 2048, 512], P('depth', 'dp')
All inputs are finite; a program needn't handle non-finite values.
Results may differ from a plain program's by a relative error of at most 0.03.
Values may be sent and summed in bfloat16 or wider, within the bound.
A program may use at most 64 MiB of HBM per device.

v0:
```python
import jax
import jax.numpy as jnp
from jax import lax
from jax.sharding import PartitionSpec as P

RELAX = 3
EPSILON = 1e-06
GAMMA = 0.05


def shifted(block, axis, distance):
    devices = range(lax.axis_size(axis))
    route = [(i - distance, i) for i in devices if i - distance in devices]
    return lax.ppermute(block, axis, route)


def layer_forward(state, weight_up, weight_down):
    scale = lax.rsqrt(jnp.mean(state * state, axis=-1, keepdims=True) + EPSILON)
    normed = (state * scale).astype(jnp.bfloat16)
    before = jnp.dot(normed, weight_up, preferred_element_type=jnp.float32)
    hidden = jax.nn.silu(before).astype(jnp.bfloat16)
    output = state + jnp.dot(hidden, weight_down, preferred_element_type=jnp.float32)
    return (output, (scale, normed, before, hidden))


def layer_adjoint(state, saved, adjoint, weight_up, weight_down):
    scale, normed, before, hidden = saved
    adjoint_low = adjoint.astype(jnp.bfloat16)
    toward_hidden = lax.dot_general(
        adjoint_low, weight_down, (((1,), (1,)), ((), ())), preferred_element_type=jnp.float32
    )
    sigma = jax.nn.sigmoid(before)
    delta = (toward_hidden * sigma * (1.0 + before * (1.0 - sigma))).astype(jnp.bfloat16)
    toward_normed = lax.dot_general(
        delta, weight_up, (((1,), (1,)), ((), ())), preferred_element_type=jnp.float32
    )
    unit = state * scale
    inner = jnp.mean(toward_normed * unit, axis=-1, keepdims=True)
    return (adjoint + scale * (toward_normed - unit * inner), adjoint_low, delta)


def coarse_matrix(weight_up, weight_down):
    total = jnp.dot(weight_up[0], weight_down[0], preferred_element_type=jnp.float32)
    total = total + jnp.dot(weight_up[1], weight_down[1], preferred_element_type=jnp.float32)
    return jnp.eye(weight_up.shape[1], dtype=jnp.float32) + GAMMA * total


def shards(token_ids, embedding, w_up, w_down, cotangent):
    depth = lax.axis_size("depth")
    position = lax.axis_index("depth")
    first = position == 0
    final_block = position == depth - 1
    layers = w_up.shape[0]
    vocab_rows = embedding.shape[0]
    local_ids = token_ids - position * vocab_rows
    inside = (local_ids >= 0) & (local_ids < vocab_rows)
    picked = jnp.take(embedding, jnp.clip(local_ids, 0, vocab_rows - 1), axis=0)
    picked = jnp.where(inside[:, None], picked, jnp.zeros_like(picked)).astype(jnp.float32)
    start = lax.psum(picked.astype(jnp.bfloat16), "depth").astype(jnp.float32)
    matrix = coarse_matrix(w_up, w_down)
    transposed = matrix.T
    zeros = jnp.zeros_like(start)
    coarse = start
    arrived_projection = zeros
    for sweep in range(RELAX):
        run_state = coarse
        for run_layer in range(layers):
            run_state, unused = layer_forward(run_state, w_up[run_layer], w_down[run_layer])
        projection = jnp.dot(coarse, matrix, precision=lax.Precision.HIGHEST)
        arrived, arrived_projection = shifted((run_state, projection), "depth", 1)
        coarse = jnp.where(first, start, arrived)
    tau = coarse - arrived_projection

    def forward_turn(turn, incoming):
        carried = jnp.dot(incoming + tau, matrix, precision=lax.Precision.HIGHEST)
        return shifted(carried.astype(jnp.bfloat16), "depth", 1).astype(carried.dtype)

    incoming = lax.fori_loop(0, depth - 1, forward_turn, zeros)
    corrected = incoming + tau
    states = []
    saves = []
    state = corrected
    for layer in range(layers):
        states.append(state)
        state, saved = layer_forward(state, w_up[layer], w_down[layer])
        saves.append(saved)

    def run_adjoint(adjoint):
        for layer in reversed(range(layers)):
            adjoint, low, delta = layer_adjoint(
                states[layer], saves[layer], adjoint, w_up[layer], w_down[layer]
            )
        return adjoint

    final = cotangent.astype(jnp.float32)
    adjoint_state = final
    back_projection = zeros
    for sweep in range(RELAX):
        begun = run_adjoint(adjoint_state)
        projection = jnp.dot(adjoint_state, transposed, precision=lax.Precision.HIGHEST)
        arrived, back_projection = (
            shifted(begun.astype(jnp.bfloat16), "depth", -1).astype(begun.dtype),
            shifted(projection.astype(jnp.bfloat16), "depth", -1).astype(projection.dtype),
        )
        adjoint_state = jnp.where(final_block, final, arrived)
    back_tau = adjoint_state - back_projection

    def backward_turn(turn, incoming):
        carried = jnp.dot(incoming + back_tau, transposed, precision=lax.Precision.HIGHEST)
        return shifted(carried.astype(jnp.bfloat16), "depth", -1).astype(carried.dtype)

    back_incoming = lax.fori_loop(0, depth - 1, backward_turn, zeros)
    adjoint = back_incoming + back_tau
    lows = [None] * layers
    deltas = [None] * layers
    for layer in reversed(range(layers)):
        adjoint, low, delta = layer_adjoint(
            states[layer], saves[layer], adjoint, w_up[layer], w_down[layer]
        )
        lows[layer] = low
        deltas[layer] = delta
    local_up = jnp.stack(
        [
            lax.dot_general(
                saves[layer][1],
                deltas[layer],
                (((0,), (0,)), ((), ())),
                preferred_element_type=jnp.float32,
            )
            for layer in range(layers)
        ],
        0,
    )
    local_down = jnp.stack(
        [
            lax.dot_general(
                saves[layer][3],
                lows[layer],
                (((0,), (0,)), ((), ())),
                preferred_element_type=jnp.float32,
            )
            for layer in range(layers)
        ],
        0,
    )
    grad_up, grad_down = (
        lax.psum_scatter(
            local_up.astype(jnp.bfloat16), "dp", scatter_dimension=1, tiled=True
        ).astype(jnp.float32),
        lax.psum_scatter(
            local_down.astype(jnp.bfloat16), "dp", scatter_dimension=1, tiled=True
        ).astype(jnp.float32),
    )
    return (grad_up, grad_down)


def solution(mesh):
    in_specs = (
        P("dp"),
        P("depth", None),
        P("depth", None, None),
        P("depth", None, None),
        P("dp", None),
    )
    out_specs = (P("depth", "dp", None), P("depth", "dp", None))
    return jax.shard_map(shards, mesh=mesh, in_specs=in_specs, out_specs=out_specs, check_vma=False)
```

profile of v0, /device:TPU:8, one launch (start us, length us, event | category | flops | bytes accessed | tf_op | source)
XLA Modules:
  0.0 967.2 jit_solution(8096644310616206722)
XLA Ops:
  10.2 121.4 %all-reduce.2.cloned.1.call-done = bf16[128,512]{1,0:T(8,128)(2,1)} async-done(((bf16[128,512]{1,0:T(8,128)(2,1)}), bf16[128,512]{1,0:T(8,128)(2,1)}) %all-reduce.2.cloned.1.call-update) | async-done | bytes 131088 | tf_op jit(solution)/shard_map/psum | solution.py:59
  140.8 4.5 fusion.30
  163.6 3.8 multiply_reduce_fusion.9
  179.2 4.2 collective-permute-done.5
  184.5 119.6 %while.22 = (s32[]{:T(128)}, f32[128,512]{1,0:T(8,128)S(1)}, f32[128,512]{1,0:T(8,128)S(1)}, f32[512,512]{1,0:T(8,128)S(1)}, s32[]{:T(128)}, /*index=5*/s32[]{:T(128)}) while((s32[]{:T(128)}, f32[128,512]{1,0:T(8,128)S(1)}, f32[128,512]{1,0:T(8,128)S(1)}, f32[512,512]{1,0:T(8,128)S(1)}, s32[]{:T(128)}, /*index=5*/s32[]{:T(128)}) %tuple.59), condition=%wide.region_8.9_spmd.clone, body=%wide.region_7.8_spmd.clone.sunk | while | flops 402915328 | bytes 2621559 | solution.py:78
  187.1 4.4 collective-permute-done
  194.2 4.4 collective-permute-done
  201.3 4.4 collective-permute-done
  208.4 4.4 collective-permute-done
  215.4 4.4 collective-permute-done
  222.5 4.4 collective-permute-done
  229.6 4.3 collective-permute-done
  234.7 4.1 collective-permute-start
  241.8 6.2 collective-permute-start
  249.7 7.4 collective-permute-start
  258.9 7.4 collective-permute-start
  268.1 7.4 collective-permute-start
  277.3 7.4 collective-permute-start
  286.4 7.4 collective-permute-start
  295.6 7.4 collective-permute-start
  311.0 4.2 multiply_reduce_fusion.6
  315.2 3.9 multiply_reduce_fusion.5
  321.9 6.5 collective-permute-done.6
  328.4 4.2 multiply_reduce_fusion.4
  333.7 3.9 multiply_reduce_fusion.3
  339.6 7.2 collective-permute-done.7
  346.8 4.2 multiply_reduce_fusion.2
  351.1 4.9 multiply_reduce_fusion.1
  369.2 139.0 %while.23 = (s32[]{:T(128)}, f32[128,512]{1,0:T(8,128)S(1)}, f32[128,512]{1,0:T(8,128)S(1)}, f32[512,512]{1,0:T(8,128)S(1)}, s32[]{:T(128)}, /*index=5*/s32[]{:T(128)}) while((s32[]{:T(128)}, f32[128,512]{1,0:T(8,128)S(1)}, f32[128,512]{1,0:T(8,128)S(1)}, f32[512,512]{1,0:T(8,128)S(1)}, s32[]{:T(128)}, ...), condition=%wide.region_18.19_spmd.clone, body=%wide.region_17.18_spmd.clone.sunk | while | flops 402915328 | bytes 2621559 | solution.py:112
  371.9 7.2 collective-permute-done.1
  381.8 6.3 collective-permute-done.1
  390.8 7.2 collective-permute-done.1
  400.7 6.5 collective-permute-done.1
  409.9 6.5 collective-permute-done.1
  419.0 6.5 collective-permute-done.1
  428.2 6.5 collective-permute-done.1
  437.4 6.5 collective-permute-done.1
  446.6 6.5 collective-permute-done.1
  455.8 6.5 collective-permute-done.1
  464.9 6.5 collective-permute-done.1
  474.1 6.5 collective-permute-done.1
  483.3 6.5 collective-permute-done.1
  492.5 6.5 collective-permute-done.1
  501.7 6.5 collective-permute-done.1
  519.6 4.9 fusion.6
  524.5 3.9 pad_maximum_fusion
  528.4 219.8 %reduce-scatter.5.cloned.1.call-done = bf16[2,128,512]{2,1,0:T(8,128)(2,1)} async-done(((bf16[2,2048,512]{2,1,0:T(8,128)(2,1)}), bf16[2,128,512]{2,1,0:T(8,128)(2,1)}) %reduce-scatter.5.cloned.1.call-update) | async-done | bytes 262160 | tf_op jit(solution)/shard_map/reduce_scatter | solution.py:150
  750.0 208.9 %reduce-scatter.3.cloned.1.call-done = bf16[2,32,2048]{2,1,0:T(8,128)(2,1)} async-done(((bf16[2,512,2048]{2,1,0:T(8,128)(2,1)}), bf16[2,32,2048]{2,1,0:T(8,128)(2,1)}) %reduce-scatter.3.cloned.1.call-update) | async-done | bytes 262160 | tf_op jit(solution)/shard_map/reduce_scatter | solution.py:147
  (194 shorter events, 158.0 us)
Async XLA Ops:
  7.2 124.4 %all-reduce.2.cloned.1.call-start = ((), (), s32[]{:S(2)}) async-start(), calls=%async_computation.2 | async-start | bytes 262144 | tf_op jit(solution)/shard_map/psum | solution.py:59
  10.1 738.1 %reduce-scatter.5.cloned.1.call-start = ((), (), s32[]{:S(2)}) async-start(), calls=%async_computation.4 | async-start | bytes 4456448 | tf_op jit(solution)/shard_map/reduce_scatter | solution.py:150
  138.7 9.2 copy-start.7
  138.8 9.2 collective-permute-start.2
  154.9 7.9 collective-permute-start.3
  160.6 12.6 %copy-start.1 = (f32[512,512]{1,0:T(8,128)}, f32[512,512]{1,0:T(8,128)S(1)}, u32[]{:S(2)}) copy-start(f32[512,512]{1,0:T(8,128)S(1)} %get-tuple-element.110) | copy-start | bytes 3145732
  171.2 8.0 collective-permute-start.4
  175.6 7.9 collective-permute-start.5
  185.2 6.3 collective-permute-start
  192.3 6.3 collective-permute-start
  199.4 6.3 collective-permute-start
  206.4 6.3 collective-permute-start
  213.5 6.3 collective-permute-start
  220.6 6.3 collective-permute-start
  227.6 6.3 collective-permute-start
  234.7 6.3 collective-permute-start
  241.8 7.2 collective-permute-start
  249.7 8.4 collective-permute-start
  258.9 8.4 collective-permute-start
  268.1 8.4 collective-permute-start
  277.3 8.4 collective-permute-start
  286.4 8.4 collective-permute-start
  295.6 8.4 collective-permute-start
  304.2 51.9 %copy-start.4 = (f32[128,512]{1,0:T(8,128)}, f32[128,512]{1,0:T(8,128)S(1)}, u32[]{:S(2)}) copy-start(f32[128,512]{1,0:T(8,128)S(1)} %get-tuple-element.99) | copy-start | bytes 786436
  307.0 26.7 %copy-start.10 = (f32[128,2048]{1,0:T(8,128)}, f32[128,2048]{1,0:T(8,128)S(1)}, u32[]{:S(2)}) copy-start(f32[128,2048]{1,0:T(8,128)S(1)} %fusion.75) | copy-start | bytes 3145732
  319.9 8.4 collective-permute-start.6
  328.4 4.2 copy-start.13
  337.7 9.1 collective-permute-start.7
  351.1 8.6 copy-start.2
  357.8 8.5 collective-permute-start.8
  360.9 8.3 collective-permute-start.9
  369.9 9.1 collective-permute-start.1
  379.8 8.3 collective-permute-start.1
  388.9 9.1 collective-permute-start.1
  398.8 8.4 collective-permute-start.1
  408.0 8.4 collective-permute-start.1
  417.1 8.4 collective-permute-start.1
  426.3 8.4 collective-permute-start.1
  435.5 8.4 collective-permute-start.1
  444.7 8.4 collective-permute-start.1
  453.9 8.4 collective-permute-start.1
  463.0 8.4 collective-permute-start.1
  472.2 8.4 collective-permute-start.1
  481.4 8.4 collective-permute-start.1
  490.6 8.4 collective-permute-start.1
  499.7 8.4 collective-permute-start.1
  517.4 441.5 %reduce-scatter.3.cloned.1.call-start = ((), (), s32[]{:S(2)}) async-start(), calls=%async_computation.3 | async-start | bytes 4456448 | tf_op jit(solution)/shard_map/reduce_scatter | solution.py:147
  519.6 4.9 copy-start.3
  (8 other events, 19.9 us)
Sparse Core Ops, SparseCore 0:
  11.2 120.3 all-reduce.1
  517.5 230.6 reduce-scatter.4
  752.2 206.5 reduce-scatter.2
where the time goes:
time: 969 us; the launch traced here: 967 us
  waiting for transfers between devices  716 us (74%)
  starting transfers between devices  113 us (12%)
  matrix products  96.1 us (10%)
  other arithmetic  19.6 us (2%)
  between operations  14.2 us (1%)
    reduce_scatter x1, waiting for transfers between devices, shards(): lax.psum_scatter(local_down.astype(jnp.bfloat16), 'dp', scatter_dimension...  220 us
    reduce_scatter x1, waiting for transfers between devices, shards(): lax.psum_scatter(local_up.astype(jnp.bfloat16), 'dp', scatter_dimension=1...  209 us
    ppermute x38, waiting for transfers between devices, shifted(): return lax.ppermute(block, axis, route)  166 us
    psum x1, waiting for transfers between devices, shards(): start = lax.psum(picked.astype(jnp.bfloat16), 'depth').astype(jnp.float32)  121 us
    ppermute x38, starting transfers between devices, shifted(): return lax.ppermute(block, axis, route)  113 us
    dot_general x7, matrix products, layer_adjoint(): lax.dot_general(delta, weight_up, (((1,), (1,)), ((), ())), preferred_ele...  26.2 us
    dot_general x7, matrix products, layer_forward(): jnp.dot(hidden, weight_down, preferred_element_type=jnp.float32)  21.1 us
  transfers between devices with their start and end apart: 41, of which 41 were waited for; matrix products, arithmetic and copies ran while one was open for 3% of the time, Pallas kernels for 0%

commit v1 on v0

--- a/solution.py
+++ b/solution.py
@@ -6,6 +6,12 @@
 RELAX = 3
 EPSILON = 1e-06
 GAMMA = 0.05
+
+
+def deliver_teams(piece_in):
+    val2 = jax.lax.all_gather(piece_in, "depth")
+    local_part = jnp.sum(val2, axis=0)
+    return local_part
 
 
 def shifted(block, axis, distance):
@@ -56,7 +62,7 @@
     inside = (local_ids >= 0) & (local_ids < vocab_rows)
     picked = jnp.take(embedding, jnp.clip(local_ids, 0, vocab_rows - 1), axis=0)
     picked = jnp.where(inside[:, None], picked, jnp.zeros_like(picked)).astype(jnp.float32)
-    start = lax.psum(picked.astype(jnp.bfloat16), "depth").astype(jnp.float32)
+    start = deliver_teams(picked.astype(jnp.bfloat16)).astype(jnp.float32)
     matrix = coarse_matrix(w_up, w_down)
     transposed = matrix.T
     zeros = jnp.zeros_like(start)

time: 969 us -> 885 us (0.913)
  waiting for transfers between devices: 716 us -> 633 us
    psum x1 -> x0, waiting for transfers between devices: 121 us -> none  [shards(): start = lax.psum(picked.astype(jnp.bfloat16), 'depth').astype(jnp.float32)]
    all_gather x0 -> x1, waiting for transfers between devices: none -> 39.3 us  [deliver_teams(): val2 = jax.lax.all_gather(piece_in, 'depth')]
where the time goes in v1:
time: 885 us; the launch traced here: 884 us
  waiting for transfers between devices  633 us (72%)
  starting transfers between devices  111 us (13%)
  matrix products  96.1 us (11%)
  other arithmetic  20.6 us (2%)
  between operations  14.2 us (2%)
    reduce_scatter x1, waiting for transfers between devices, shards(): lax.psum_scatter(local_down.astype(jnp.bfloat16), 'dp', scatter_dimension...  220 us
    reduce_scatter x1, waiting for transfers between devices, shards(): lax.psum_scatter(local_up.astype(jnp.bfloat16), 'dp', scatter_dimension=1...  209 us
    ppermute x38, waiting for transfers between devices, shifted(): return lax.ppermute(block, axis, route)  165 us
    ppermute x38, starting transfers between devices, shifted(): return lax.ppermute(block, axis, route)  111 us
    all_gather x1, waiting for transfers between devices, deliver_teams(): val2 = jax.lax.all_gather(piece_in, 'depth')  39.3 us
    dot_general x7, matrix products, layer_adjoint(): lax.dot_general(delta, weight_up, (((1,), (1,)), ((), ())), preferred_ele...  26.2 us
    dot_general x7, matrix products, layer_forward(): jnp.dot(hidden, weight_down, preferred_element_type=jnp.float32)  21.1 us
  transfers between devices with their start and end apart: 41, of which 41 were waited for; matrix products, arithmetic and copies ran while one was open for 3% of the time, Pallas kernels for 0%

profile of v1, /device:TPU:8, one launch (start us, length us, event | category | flops | bytes accessed | tf_op | source)
XLA Modules:
  0.0 883.6 jit_solution(10207585350663441745)
XLA Ops:
  10.2 39.3 %all-gather.2.cloned.1.call-done = bf16[16,128,512]{2,1,0:T(8,128)(2,1)} async-done(((bf16[1,128,512]{2,1,0:T(8,128)(2,1)}), bf16[16,128,512]{2,1,0:T(8,128)(2,1)}) %all-gather.2.cloned.1.call-update) | async-done | bytes 2097168 | tf_op jit(solution)/shard_map/all_gather | solution.py:12
  59.8 4.5 fusion.30
  81.0 3.8 multiply_reduce_fusion.9
  84.8 3.8 fusion.124
  96.6 4.2 collective-permute-done.5
  101.8 118.2 %while.22 = (s32[]{:T(128)}, f32[128,512]{1,0:T(8,128)S(1)}, f32[128,512]{1,0:T(8,128)S(1)}, f32[512,512]{1,0:T(8,128)S(1)}, s32[]{:T(128)}, /*index=5*/s32[]{:T(128)}) while((s32[]{:T(128)}, f32[128,512]{1,0:T(8,128)S(1)}, f32[128,512]{1,0:T(8,128)S(1)}, f32[512,512]{1,0:T(8,128)S(1)}, s32[]{:T(128)}, /*index=5*/s32[]{:T(128)}) %tuple.60), condition=%wide.region_8.9_spmd.clone, body=%wide.region_7.8_spmd.clone.sunk | while | flops 402915328 | bytes 2621559 | solution.py:84
  104.5 4.4 collective-permute-done
  111.6 4.4 collective-permute-done
  118.6 4.4 collective-permute-done
  125.7 4.4 collective-permute-done
  132.8 4.4 collective-permute-done
  139.9 4.4 collective-permute-done
  146.9 4.4 collective-permute-done
  159.1 4.8 collective-permute-start
  166.2 6.9 collective-permute-start
  174.9 7.4 collective-permute-start
  184.1 7.4 collective-permute-start
  193.3 7.4 collective-permute-start
  202.4 7.4 collective-permute-start
  211.6 7.4 collective-permute-start
  227.0 4.2 multiply_reduce_fusion.6
  231.2 3.9 multiply_reduce_fusion.5
  237.8 6.5 collective-permute-done.6
  244.4 4.2 multiply_reduce_fusion.4
  249.7 3.9 multiply_reduce_fusion.3
  255.6 7.2 collective-permute-done.7
  262.8 4.2 multiply_reduce_fusion.2
  267.1 4.9 multiply_reduce_fusion.1
  285.2 139.0 %while.23 = (s32[]{:T(128)}, f32[128,512]{1,0:T(8,128)S(1)}, f32[128,512]{1,0:T(8,128)S(1)}, f32[512,512]{1,0:T(8,128)S(1)}, s32[]{:T(128)}, /*index=5*/s32[]{:T(128)}) while((s32[]{:T(128)}, f32[128,512]{1,0:T(8,128)S(1)}, f32[128,512]{1,0:T(8,128)S(1)}, f32[512,512]{1,0:T(8,128)S(1)}, s32[]{:T(128)}, ...), condition=%wide.region_18.19_spmd.clone, body=%wide.region_17.18_spmd.clone.sunk | while | flops 402915328 | bytes 2621559 | solution.py:118
  287.8 7.2 collective-permute-done.1
  297.7 6.3 collective-permute-done.1
  306.8 7.2 collective-permute-done.1
  316.7 6.5 collective-permute-done.1
  325.9 6.5 collective-permute-done.1
  335.0 6.5 collective-permute-done.1
  344.2 6.5 collective-permute-done.1
  353.4 6.5 collective-permute-done.1
  362.6 6.5 collective-permute-done.1
  371.8 6.5 collective-permute-done.1
  380.9 6.5 collective-permute-done.1
  390.1 6.5 collective-permute-done.1
  399.3 6.5 collective-permute-done.1
  408.5 6.5 collective-permute-done.1
  417.6 6.5 collective-permute-done.1
  435.6 4.9 fusion.6
  440.5 3.9 pad_maximum_fusion
  444.4 219.7 %reduce-scatter.5.cloned.1.call-done = bf16[2,128,512]{2,1,0:T(8,128)(2,1)} async-done(((bf16[2,2048,512]{2,1,0:T(8,128)(2,1)}), bf16[2,128,512]{2,1,0:T(8,128)(2,1)}) %reduce-scatter.5.cloned.1.call-update) | async-done | bytes 262160 | tf_op jit(solution)/shard_map/reduce_scatter | solution.py:156
  665.9 209.5 %reduce-scatter.3.cloned.1.call-done = bf16[2,32,2048]{2,1,0:T(8,128)(2,1)} async-done(((bf16[2,512,2048]{2,1,0:T(8,128)(2,1)}), bf16[2,32,2048]{2,1,0:T(8,128)(2,1)}) %reduce-scatter.3.cloned.1.call-update) | async-done | bytes 262160 | tf_op jit(solution)/shard_map/reduce_scatter | solution.py:153
  (193 shorter events, 158.2 us)
Async XLA Ops:
  7.2 42.3 %all-gather.2.cloned.1.call-start = ((), (), s32[]{:S(2)}) async-start(), calls=%async_computation.2 | async-start | bytes 2228224 | tf_op jit(solution)/shard_map/all_gather | solution.py:12
  10.1 653.9 %reduce-scatter.5.cloned.1.call-start = ((), (), s32[]{:S(2)}) async-start(), calls=%async_computation.4 | async-start | bytes 4456448 | tf_op jit(solution)/shard_map/reduce_scatter | solution.py:156
  57.7 7.7 collective-permute-start.2
  72.3 7.9 collective-permute-start.3
  77.9 12.6 %copy-start.1 = (f32[512,512]{1,0:T(8,128)}, f32[512,512]{1,0:T(8,128)S(1)}, u32[]{:S(2)}) copy-start(f32[512,512]{1,0:T(8,128)S(1)} %get-tuple-element.114) | copy-start | bytes 3145732
  88.6 8.0 collective-permute-start.4
  92.9 7.9 collective-permute-start.5
  102.6 6.3 collective-permute-start
  109.6 6.3 collective-permute-start
  116.7 6.3 collective-permute-start
  123.8 6.3 collective-permute-start
  130.9 6.3 collective-permute-start
  137.9 6.3 collective-permute-start
  145.0 6.3 collective-permute-start
  152.1 6.3 collective-permute-start
  159.1 6.3 collective-permute-start
  166.2 7.9 collective-permute-start
  174.9 8.4 collective-permute-start
  184.1 8.4 collective-permute-start
  193.3 8.4 collective-permute-start
  202.4 8.4 collective-permute-start
  211.6 8.4 collective-permute-start
  220.2 51.9 %copy-start.4 = (f32[128,512]{1,0:T(8,128)}, f32[128,512]{1,0:T(8,128)S(1)}, u32[]{:S(2)}) copy-start(f32[128,512]{1,0:T(8,128)S(1)} %get-tuple-element.103) | copy-start | bytes 786436
  223.0 26.7 %copy-start.9 = (f32[128,2048]{1,0:T(8,128)}, f32[128,2048]{1,0:T(8,128)S(1)}, u32[]{:S(2)}) copy-start(f32[128,2048]{1,0:T(8,128)S(1)} %fusion.75) | copy-start | bytes 3145732
  223.0 4.1 copy-start.7
  235.9 8.4 collective-permute-start.6
  244.4 4.2 copy-start.12
  253.7 9.1 %collective-permute-start.7 = (bf16[128,512]{1,0:T(8,128)(2,1)S(1)}, bf16[128,512]{1,0:T(8,128)(2,1)S(1)}, u32[]{:S(2)}, u32[]{:S(2)}) collective-permute-start(bf16[128,512]{1,0:T(8,128)(2,1)S(1)} %add_convert_fusion.2), channel_id=1, source_target_pairs={{16,0},{32,16},{48,32},{64,48},{80,64},{96,80},{112,96},{128,112},... | collective-permute-start | bytes 393224 | tf_op jit(solution)/shard_map/ppermute | solution.py:20
  267.1 8.6 copy-start.2
  273.8 8.5 collective-permute-start.8
  276.9 8.3 collective-permute-start.9
  285.9 9.1 %collective-permute-start.1 = (bf16[128,512]{1,0:T(8,128)(2,1)S(1)}, bf16[128,512]{1,0:T(8,128)(2,1)S(1)}, u32[]{:S(2)}, u32[]{:S(2)}) collective-permute-start(bf16[128,512]{1,0:T(8,128)(2,1)S(1)} %convolution_convert_fusion.10), channel_id=1, source_target_pairs={{16,0},{32,16},{48,32},{64,48},{80,64},{96,80},{112,96},{128,112},... | collective-permute-start | bytes 393224 | tf_op jit(solution)/shard_map/while/body/eval_jaxpr/ppermute | solution.py:20
  295.8 8.3 collective-permute-start.1
  304.9 9.1 %collective-permute-start.1 = (bf16[128,512]{1,0:T(8,128)(2,1)S(1)}, bf16[128,512]{1,0:T(8,128)(2,1)S(1)}, u32[]{:S(2)}, u32[]{:S(2)}) collective-permute-start(bf16[128,512]{1,0:T(8,128)(2,1)S(1)} %convolution_convert_fusion.10), channel_id=1, source_target_pairs={{16,0},{32,16},{48,32},{64,48},{80,64},{96,80},{112,96},{128,112},... | collective-permute-start | bytes 393224 | tf_op jit(solution)/shard_map/while/body/eval_jaxpr/ppermute | solution.py:20
  314.7 8.4 collective-permute-start.1
  323.9 8.4 collective-permute-start.1
  333.1 8.4 collective-permute-start.1
  342.3 8.4 collective-permute-start.1
  351.5 8.4 collective-permute-start.1
  360.6 8.4 collective-permute-start.1
  369.8 8.4 collective-permute-start.1
  379.0 8.4 collective-permute-start.1
  388.2 8.4 collective-permute-start.1
  397.4 8.4 collective-permute-start.1
  406.5 8.4 collective-permute-start.1
  415.7 8.4 collective-permute-start.1
  433.4 441.9 %reduce-scatter.3.cloned.1.call-start = ((), (), s32[]{:S(2)}) async-start(), calls=%async_computation.3 | async-start | bytes 4456448 | tf_op jit(solution)/shard_map/reduce_scatter | solution.py:153
  435.6 4.9 copy-start.3
  (7 other events, 15.8 us)
Sparse Core Ops, SparseCore 0:
  10.4 39.0 all-gather.1
  433.5 230.5 reduce-scatter.4
  668.6 206.6 reduce-scatter.2
